TPU v7x, 32 devices: a whole 2x2x4 slice. The times are simulated.
32 devices in a mesh: inv: 2 (over x), src: 2 (over core), gx: 8 (over z, y).
Axes of the slice: x: 2, y: 2, z: 4, core: 2. Of those that a mesh axis runs over, the one named last changes fastest.
Arguments:
- log_cond: float32 [64, 64, 128], P('inv', ('src', 'gx')), parts along dimension 0, may hold values from -2 to 1
- e_start: float32 [2, 6, 16, 32, 128], P('src', 'inv', 'gx'), parts along dimension 1, may hold values from -6 to 6
- offsets: int32 [2, 2], replicated, may hold values from 0 to 16, as said below
- rec_cells: int32 [2, 8192], P('src', 'gx'), may hold values from 0 to 8191, as said below
- observed: float32 [2, 8, 8192], P('src', 'inv', 'gx'), parts along dimension 1, may hold values from -6 to 6
Outputs:
- model_grad: float32 [64, 64, 128], P('inv', ('src', 'gx')), parts along dimension 0
There are 2 independent parts, one for each index of `inv`. A program takes and returns all parts, laid end to end along the dimension named above; an argument that names none is the same for every part. Nothing has to cross between parts.
Inputs may be any that keep to these rules, and one draw needn't show every extreme that they name: `offsets`: column 0 of a row is that group's first model plane along x; column 1 its first model block of 4 columns along y, at most 8. `rec_cells`: in each group, positions d * 1024 to (d + 1) * 1024 - 1 name cells of footprint planes d * 2 to (d + 1) * 2 - 1, as (x - d * 2) * 32 * 128 + y * 128 + z; cells may repeat.
All inputs are finite; a program needn't handle non-finite values.
Results may differ from a plain program's by a relative error of at most 0.00002.
Values sent between devices are 32-bit elements; how exact they have to be, the bound alone decides.
A program may use at most 64 MiB of HBM per device.

v0:
```python
import jax
import jax.numpy as jnp
from jax import lax
from jax.sharding import PartitionSpec as P

STEPS = 4


electric_step = 0.5
magnetic_step = 0.5
loss_scale = 0.25


def passed_along(value, axis, steps):
    count = lax.axis_size(axis)
    leading, last = (max(0, -steps), min(count, count - steps))
    return lax.ppermute(value, axis, [(source, source + steps) for source in range(leading, last)])


def forward_x(values, ghost):
    return jnp.concatenate([values[1:], ghost], 0) - values


def backward_x(values, ghost):
    return values - jnp.concatenate([ghost, values[:-1]], 0)


def forward_y(values):
    return jnp.pad(values[:, 1:], ((0, 0), (0, 1), (0, 0))) - values


def backward_y(values):
    return values - jnp.pad(values[:, :-1], ((0, 0), (1, 0), (0, 0)))


def forward_z(values):
    return jnp.pad(values[:, :, 1:], ((0, 0), (0, 0), (0, 1))) - values


def backward_z(values):
    return values - jnp.pad(values[:, :, :-1], ((0, 0), (0, 0), (1, 0)))


def magnetic_update(electric, magnetic, right_ghosts):
    return (
        magnetic[0] - magnetic_step * (forward_y(electric[2]) - forward_z(electric[1])),
        magnetic[1]
        - magnetic_step * (forward_z(electric[0]) - forward_x(electric[2], right_ghosts[1])),
        magnetic[2]
        - magnetic_step * (forward_x(electric[1], right_ghosts[0]) - forward_y(electric[0])),
    )


def electric_update(electric, magnetic, left_ghosts, damping, driving):
    return (
        damping * electric[0] + driving * (backward_y(magnetic[2]) - backward_z(magnetic[1])),
        damping * electric[1]
        + driving * (backward_z(magnetic[0]) - backward_x(magnetic[2], left_ghosts[1])),
        damping * electric[2]
        + driving * (backward_x(magnetic[1], left_ghosts[0]) - backward_y(magnetic[0])),
    )


def advance(electric, magnetic, damping, driving):
    right = passed_along(jnp.stack([electric[1][:1], electric[2][:1]]), "gx", -1)
    magnetic = magnetic_update(electric, magnetic, (right[0], right[1]))
    left = passed_along(jnp.stack([magnetic[1][-1:], magnetic[2][-1:]]), "gx", 1)
    electric = electric_update(electric, magnetic, (left[0], left[1]), damping, driving)
    return (electric, magnetic)


def local(log_cond, e_start, offsets, rec_cells, observed):
    groups = offsets.shape[0]
    width = lax.axis_size("gx")
    owners = lax.axis_size("src") * width
    blocks = owners // 2
    planes = e_start.shape[2]
    columns = e_start.shape[3]
    depth = e_start.shape[4]
    block_cols = log_cond.shape[1]
    foot_x = planes * width
    group = lax.axis_index("src")
    slab = lax.axis_index("gx")
    own_block = group * width + slab
    pieces = []
    for source in range(groups):
        start_block = offsets[source, 1]
        inside = ((own_block >= start_block) & (own_block < start_block + blocks)).astype(
            jnp.float32
        )
        window = lax.dynamic_slice_in_dim(log_cond, offsets[source, 0], foot_x, 0) * inside
        pieces.append(window.reshape(width, planes, block_cols, depth))
    outgoing = jnp.concatenate(pieces, 0)
    incoming = lax.all_to_all(outgoing, ("src", "gx"), split_axis=0, concat_axis=0, tiled=True)
    my_block = offsets[group, 1]
    mine = lax.dynamic_slice_in_dim(incoming, my_block, blocks, 0)
    mfoot = jnp.transpose(mine, (1, 0, 2, 3)).reshape(planes, columns, depth)
    sigma = jnp.exp(mfoot)
    absorb = loss_scale * sigma
    damping = (1.0 - absorb) / (1.0 + absorb)
    driving = electric_step / (1.0 + absorb)
    cells = rec_cells[0]
    electric = (e_start[0, 0], e_start[0, 1], e_start[0, 2])
    zero_field = jnp.zeros((planes, columns, depth), jnp.float32)
    magnetic = (zero_field, zero_field, zero_field)
    stored = []
    traces = []
    for number in range(STEPS):
        electric, magnetic = advance(electric, magnetic, damping, driving)
        stored.append(electric)
        traces.append(electric[0].reshape(-1)[cells])
    resid = jnp.stack(traces) - observed[0]
    adjoint_e = (zero_field, zero_field, zero_field)
    adjoint_h = (zero_field, zero_field, zero_field)
    total = zero_field
    for number in range(STEPS):
        adjoint_e, adjoint_h = advance(adjoint_e, adjoint_h, damping, driving)
        injected = (
            adjoint_e[0]
            .reshape(-1)
            .at[cells]
            .add(resid[STEPS - 1 - number])
            .reshape(planes, columns, depth)
        )
        adjoint_e = (injected, adjoint_e[1], adjoint_e[2])
        paired = stored[STEPS - 1 - number]
        total = total + (
            adjoint_e[0] * paired[0] + adjoint_e[1] * paired[1] + adjoint_e[2] * paired[2]
        )
    gfoot = sigma * total
    spread = jnp.transpose(gfoot.reshape(planes, blocks, block_cols, depth), (1, 0, 2, 3))
    returning = lax.dynamic_update_slice_in_dim(
        jnp.zeros((owners, planes, block_cols, depth), jnp.float32), spread, my_block, 0
    )
    arrived = lax.all_to_all(returning, ("src", "gx"), split_axis=0, concat_axis=0, tiled=True)
    model_grad = jnp.zeros(log_cond.shape, jnp.float32)
    for source in range(groups):
        contribution = arrived[source * width : (source + 1) * width].reshape(
            foot_x, block_cols, depth
        )
        start_x = offsets[source, 0]
        current = lax.dynamic_slice_in_dim(model_grad, start_x, foot_x, 0)
        model_grad = lax.dynamic_update_slice_in_dim(model_grad, current + contribution, start_x, 0)
    return model_grad


def solution(mesh):
    placed = (
        P("inv", ("src", "gx"), None),
        P("src", "inv", "gx", None, None),
        P(),
        P("src", "gx"),
        P("src", "inv", "gx"),
    )
    return jax.shard_map(
        local, mesh=mesh, in_specs=placed, out_specs=P("inv", ("src", "gx"), None), check_vma=False
    )
```

profile of v0, /device:TPU:0, one launch (start us, length us, event | category | flops | bytes accessed | tf_op | source)
XLA Modules:
  0.0 149.8 jit_solution(17478529411888844634)
XLA Ops:
  0.0 1.5 %fusion.124 = (s32[1,1]{1,0:T(1,128)}, s32[1,1]{1,0:T(1,128)}, s32[1,1]{1,0:T(1,128)}, s32[1,1]{1,0:T(1,128)}, s32[1,1]{1,0:T(1,128)}) fusion(s32[2,2]{1,0:T(2,128)} %param.7, s32[]{:T(128)S(6)} %select_n.35), kind=kLoop, calls=%fused_computation.276 | loop fusion | bytes 44 | tf_op jit(solution)/shard_map/slice | solution.py:87
  8.0 0.6 pad_maximum_fusion
  8.6 7.4 %all-to-all-start = ((f32[16,2,4,128]{3,2,1,0:T(4,128)}), f32[16,2,4,128]{3,2,1,0:T(4,128)S(1)}, u32[]{:S(2)}, u32[]{:S(2)}) async-start(f32[16,2,4,128]{3,2,1,0:T(4,128)} %pad_maximum_fusion), calls=%async_computation | async-start | bytes 131072 | tf_op jit(solution)/shard_map/all_to_all | solution.py:94
  16.1 1.3 collective-permute-start.1
  17.4 1.3 collective-permute-start
  20.7 1.3 collective-permute-done.1
  22.0 4.6 %collective-permute-start.2 = (f32[2,1,32,128]{3,2,1,0:T(8,128)S(1)}, f32[2,1,32,128]{3,2,1,0:T(8,128)S(1)}, u32[]{:S(2)}, u32[]{:S(2)}) collective-permute-start(f32[2,1,32,128]{3,2,1,0:T(8,128)S(1)} %pad_maximum_fusion.2), channel_id=1, source_target_pairs={{0,1},{1,2},{2,3},{3,4},{4,5},{5,6},{6,7},{8,9},{9,10},{10,11},{11... | collective-permute-start | bytes 98312 | tf_op jit(solution)/shard_map/ppermute | solution.py:17
  26.7 0.1 multiply_subtract_fusion.4
  26.8 4.1 %collective-permute-start.8 = (f32[2,1,32,128]{3,2,1,0:T(8,128)S(1)}, f32[2,1,32,128]{3,2,1,0:T(8,128)S(1)}, u32[]{:S(2)}, u32[]{:S(2)}) collective-permute-start(f32[2,1,32,128]{3,2,1,0:T(8,128)S(1)} %pad_maximum_fusion.8), channel_id=1, source_target_pairs={{0,1},{1,2},{2,3},{3,4},{4,5},{5,6},{6,7},{8,9},{9,10},{10,11},{11... | collective-permute-start | bytes 98312 | tf_op jit(solution)/shard_map/ppermute | solution.py:17
  30.9 1.6 %collective-permute-done.8 = f32[2,1,32,128]{3,2,1,0:T(8,128)S(1)} collective-permute-done((f32[2,1,32,128]{3,2,1,0:T(8,128)S(1)}, f32[2,1,32,128]{3,2,1,0:T(8,128)S(1)}, u32[]{:S(2)}, u32[]{:S(2)}) %collective-permute-start.8) | collective-permute-done | bytes 32800 | tf_op jit(solution)/shard_map/ppermute | solution.py:17
  32.5 0.1 multiply_add_fusion.6
  32.6 1.3 collective-permute-start.3
  33.9 0.1 multiply_add_fusion.7
  34.2 4.5 %collective-permute-done.3 = f32[2,1,32,128]{3,2,1,0:T(8,128)S(1)} collective-permute-done((f32[2,1,32,128]{3,2,1,0:T(8,128)S(1)}, f32[2,1,32,128]{3,2,1,0:T(8,128)S(1)}, u32[]{:S(2)}, u32[]{:S(2)}) %collective-permute-start.3) | collective-permute-done | bytes 32800 | tf_op jit(solution)/shard_map/ppermute | solution.py:17
  38.8 4.8 %collective-permute-start.4 = (f32[2,1,32,128]{3,2,1,0:T(8,128)S(1)}, f32[2,1,32,128]{3,2,1,0:T(8,128)S(1)}, u32[]{:S(2)}, u32[]{:S(2)}) collective-permute-start(f32[2,1,32,128]{3,2,1,0:T(8,128)S(1)} %pad_maximum_fusion.4), channel_id=1, source_target_pairs={{0,1},{1,2},{2,3},{3,4},{4,5},{5,6},{6,7},{8,9},{9,10},{10,11},{11... | collective-permute-start | bytes 98312 | tf_op jit(solution)/shard_map/ppermute | solution.py:17
  43.7 1.6 %collective-permute-done.4 = f32[2,1,32,128]{3,2,1,0:T(8,128)S(1)} collective-permute-done((f32[2,1,32,128]{3,2,1,0:T(8,128)S(1)}, f32[2,1,32,128]{3,2,1,0:T(8,128)S(1)}, u32[]{:S(2)}, u32[]{:S(2)}) %collective-permute-start.4) | collective-permute-done | bytes 32800 | tf_op jit(solution)/shard_map/ppermute | solution.py:17
  45.2 0.1 multiply_add_fusion.5
  45.4 1.3 collective-permute-start.5
  46.9 4.6 %collective-permute-done.5 = f32[2,1,32,128]{3,2,1,0:T(8,128)S(1)} collective-permute-done((f32[2,1,32,128]{3,2,1,0:T(8,128)S(1)}, f32[2,1,32,128]{3,2,1,0:T(8,128)S(1)}, u32[]{:S(2)}, u32[]{:S(2)}) %collective-permute-start.5) | collective-permute-done | bytes 32800 | tf_op jit(solution)/shard_map/ppermute | solution.py:17
  51.6 4.9 %collective-permute-start.6 = (f32[2,1,32,128]{3,2,1,0:T(8,128)S(1)}, f32[2,1,32,128]{3,2,1,0:T(8,128)S(1)}, u32[]{:S(2)}, u32[]{:S(2)}) collective-permute-start(f32[2,1,32,128]{3,2,1,0:T(8,128)S(1)} %pad_maximum_fusion.6), channel_id=1, source_target_pairs={{0,1},{1,2},{2,3},{3,4},{4,5},{5,6},{6,7},{8,9},{9,10},{10,11},{11... | collective-permute-start | bytes 98312 | tf_op jit(solution)/shard_map/ppermute | solution.py:17
  56.6 1.3 collective-permute-start.10
  57.9 6.2 %gather_fusion = f32[1024]{0:T(1024)S(1)} fusion(f32[8192]{0:T(1024)S(1)} %bitcast.243, s32[1024]{0:T(1024)S(1)} %broadcast_clamp_fusion), kind=kCustom, calls=%fused_computation | custom fusion | bytes 12288 | tf_op jit(solution)/shard_map/gather | solution.py:111
  64.1 0.1 multiply_add_fusion.4
  64.2 1.3 collective-permute-start.7
  65.5 6.2 %gather_fusion.1 = f32[1024]{0:T(1024)S(1)} fusion(f32[8192]{0:T(1024)S(1)} %bitcast.244, s32[1024]{0:T(1024)S(1)} %broadcast_clamp_fusion), kind=kCustom, calls=%fused_computation.1 | custom fusion | bytes 12288 | tf_op jit(solution)/shard_map/gather | solution.py:111
  71.9 6.2 %gather_fusion.2 = f32[1024]{0:T(1024)S(1)} fusion(f32[8192]{0:T(1024)S(1)} %bitcast.245, s32[1024]{0:T(1024)S(1)} %broadcast_clamp_fusion), kind=kCustom, calls=%fused_computation.2 | custom fusion | bytes 12288 | tf_op jit(solution)/shard_map/gather | solution.py:111
  78.1 0.1 multiply_add_fusion.3
  78.2 6.2 %gather_fusion.3 = f32[1024]{0:T(1024)S(1)} fusion(f32[8192]{0:T(1024)S(1)} %bitcast.248, s32[1024]{0:T(1024)S(1)} %broadcast_clamp_fusion), kind=kCustom, calls=%fused_computation.3 | custom fusion | bytes 12288 | tf_op jit(solution)/shard_map/gather | solution.py:111
  84.4 6.1 %scatter_fusion = f32[8192]{0:T(1024)S(1)} fusion(f32[8192]{0:T(1024)S(1)} %bitcast.225, s32[1024]{0:T(1024)S(1)} %bitcast.293, f32[1024]{0:T(1024)S(1)} %bitcast.304), kind=kCustom, calls=%fused_computation.4 | custom fusion | flops 1024 | bytes 16384 | tf_op jit(solution)/shard_map/scatter-add | solution.py:122
  90.6 0.1 multiply_subtract_fusion.2
  90.7 5.2 %collective-permute-start.11 = (f32[2,1,32,128]{3,2,1,0:T(8,128)S(1)}, f32[2,1,32,128]{3,2,1,0:T(8,128)S(1)}, u32[]{:S(2)}, u32[]{:S(2)}) collective-permute-start(f32[2,1,32,128]{3,2,1,0:T(8,128)S(1)} %pad_maximum_fusion.11), channel_id=1, source_target_pairs={{0,1},{1,2},{2,3},{3,4},{4,5},{5,6},{6,7},{8,9},{9,10},{10,11},{11... | collective-permute-start | bytes 98312 | tf_op jit(solution)/shard_map/ppermute | solution.py:17
  95.9 1.7 %collective-permute-done.11 = f32[2,1,32,128]{3,2,1,0:T(8,128)S(1)} collective-permute-done((f32[2,1,32,128]{3,2,1,0:T(8,128)S(1)}, f32[2,1,32,128]{3,2,1,0:T(8,128)S(1)}, u32[]{:S(2)}, u32[]{:S(2)}) %collective-permute-start.11) | collective-permute-done | bytes 32800 | tf_op jit(solution)/shard_map/ppermute | solution.py:17
  97.7 0.1 multiply_add_fusion.2
  97.8 1.3 collective-permute-start.12
  99.1 6.1 %scatter_fusion.1 = f32[8192]{0:T(1024)S(1)} fusion(f32[8192]{0:T(1024)S(1)} %bitcast.237, s32[1024]{0:T(1024)S(1)} %bitcast.294, f32[1024]{0:T(1024)S(1)} %bitcast.303), kind=kCustom, calls=%fused_computation.5 | custom fusion | flops 1024 | bytes 16384 | tf_op jit(solution)/shard_map/scatter-add | solution.py:122
  105.5 5.3 %collective-permute-start.13 = (f32[2,1,32,128]{3,2,1,0:T(8,128)S(1)}, f32[2,1,32,128]{3,2,1,0:T(8,128)S(1)}, u32[]{:S(2)}, u32[]{:S(2)}) collective-permute-start(f32[2,1,32,128]{3,2,1,0:T(8,128)S(1)} %pad_maximum_fusion.13), channel_id=1, source_target_pairs={{0,1},{1,2},{2,3},{3,4},{4,5},{5,6},{6,7},{8,9},{9,10},{10,11},{11... | collective-permute-start | bytes 98312 | tf_op jit(solution)/shard_map/ppermute | solution.py:17
  110.8 5.1 %collective-permute-start.9 = (f32[2,1,32,128]{3,2,1,0:T(8,128)S(1)}, f32[2,1,32,128]{3,2,1,0:T(8,128)S(1)}, u32[]{:S(2)}, u32[]{:S(2)}) collective-permute-start(f32[2,1,32,128]{3,2,1,0:T(8,128)S(1)} %pad_maximum_fusion.9), channel_id=1, source_target_pairs={{0,1},{1,2},{2,3},{3,4},{4,5},{5,6},{6,7},{8,9},{9,10},{10,11},{11... | collective-permute-start | bytes 98312 | tf_op jit(solution)/shard_map/ppermute | solution.py:17
  116.0 0.1 multiply_add_fusion.1
  116.1 1.3 collective-permute-start.14
  117.4 0.1 collective-permute-done.9
  117.5 6.1 %scatter_fusion.2 = f32[8192]{0:T(1024)S(1)} fusion(f32[8192]{0:T(1024)S(1)} %bitcast.231, s32[1024]{0:T(1024)S(1)} %bitcast.295, f32[1024]{0:T(1024)S(1)} %bitcast.302), kind=kCustom, calls=%fused_computation.6 | custom fusion | flops 1024 | bytes 16384 | tf_op jit(solution)/shard_map/scatter-add | solution.py:122
  123.9 4.5 %collective-permute-start.15 = (f32[2,1,32,128]{3,2,1,0:T(8,128)S(1)}, f32[2,1,32,128]{3,2,1,0:T(8,128)S(1)}, u32[]{:S(2)}, u32[]{:S(2)}) collective-permute-start(f32[2,1,32,128]{3,2,1,0:T(8,128)S(1)} %pad_maximum_fusion.15), channel_id=1, source_target_pairs={{0,1},{1,2},{2,3},{3,4},{4,5},{5,6},{6,7},{8,9},{9,10},{10,11},{11... | collective-permute-start | bytes 98312 | tf_op jit(solution)/shard_map/ppermute | solution.py:17
  128.4 0.1 multiply_add_fusion
  128.4 6.1 %scatter_fusion.3 = f32[8192]{0:T(1024)S(1)} fusion(f32[8192]{0:T(1024)S(1)} %bitcast.246, s32[1024]{0:T(1024)S(1)} %bitcast.296, f32[1024]{0:T(1024)S(1)} %bitcast.301), kind=kCustom, calls=%fused_computation.7 | custom fusion | flops 1024 | bytes 16384 | tf_op jit(solution)/shard_map/scatter-add | solution.py:122
  134.6 0.2 fusion.54
  134.8 13.0 %all_to_all.10 = f32[16,2,4,128]{3,2,1,0:T(4,128)S(1)} all-to-all(f32[16,2,4,128]{3,2,1,0:T(4,128)S(1)} %copy_dynamic-update-slice_fusion), channel_id=1, replica_groups=mesh['inv'=2,'src'=2,'gx'=8] {'src','gx'}, dimensions={0} | all-to-all | bytes 131072 | tf_op jit(solution)/shard_map/all_to_all | solution.py:135
  147.8 0.6 copy-done.1
  148.5 1.4 constant_dynamic-update-slice_fusion
  (129 shorter events, 1.8 us)
Async XLA Ops:
  0.0 7.9 %copy-start.2 = (f32[32,4,128]{2,1,0:T(4,128)S(1)}, f32[32,4,128]{2,1,0:T(4,128)}, u32[]{:S(2)}) copy-start(f32[32,4,128]{2,1,0:T(4,128)} %param.5) | copy-start | bytes 196612
  8.0 8.1 %copy-start = (f32[1,3,2,32,128]{4,3,2,1,0:T(8,128)S(1)}, f32[1,3,2,32,128]{4,3,2,1,0:T(8,128)}, u32[]{:S(2)}) copy-start(f32[1,3,2,32,128]{4,3,2,1,0:T(8,128)} %param.6) | copy-start | bytes 294916
  8.6 23.8 %all-to-all-start = ((f32[16,2,4,128]{3,2,1,0:T(4,128)}), f32[16,2,4,128]{3,2,1,0:T(4,128)S(1)}, u32[]{:S(2)}, u32[]{:S(2)}) async-start(f32[16,2,4,128]{3,2,1,0:T(4,128)} %pad_maximum_fusion), calls=%async_computation | async-start | bytes 131072 | tf_op jit(solution)/shard_map/all_to_all | solution.py:94
  16.1 5.9 %collective-permute-start.1 = (f32[2,1,32,128]{3,2,1,0:T(8,128)S(1)}, f32[2,1,32,128]{3,2,1,0:T(8,128)S(1)}, u32[]{:S(2)}, u32[]{:S(2)}) collective-permute-start(f32[2,1,32,128]{3,2,1,0:T(8,128)S(1)} %pad_maximum_fusion.1), channel_id=1, source_target_pairs={{1,0},{2,1},{3,2},{4,3},{5,4},{6,5},{7,6},{9,8},{10,9},{11,10},{12... | collective-permute-start | bytes 98312 | tf_op jit(solution)/shard_map/ppermute | solution.py:17
  17.4 1.3 copy-start.4
  17.4 9.3 %collective-permute-start = (f32[2,1,32,128]{3,2,1,0:T(8,128)S(1)}, f32[2,1,32,128]{3,2,1,0:T(8,128)S(1)}, u32[]{:S(2)}, u32[]{:S(2)}) collective-permute-start(f32[2,1,32,128]{3,2,1,0:T(8,128)S(1)} %stack.153), channel_id=1, source_target_pairs={{1,0},{2,1},{3,2},{4,3},{5,4},{6,5},{7,6},{9,8},{10,9},{11,10},{12... | collective-permute-start | bytes 98312 | tf_op jit(solution)/shard_map/ppermute | solution.py:17
  22.0 8.9 %collective-permute-start.2 = (f32[2,1,32,128]{3,2,1,0:T(8,128)S(1)}, f32[2,1,32,128]{3,2,1,0:T(8,128)S(1)}, u32[]{:S(2)}, u32[]{:S(2)}) collective-permute-start(f32[2,1,32,128]{3,2,1,0:T(8,128)S(1)} %pad_maximum_fusion.2), channel_id=1, source_target_pairs={{0,1},{1,2},{2,3},{3,4},{4,5},{5,6},{6,7},{8,9},{9,10},{10,11},{11... | collective-permute-start | bytes 98312 | tf_op jit(solution)/shard_map/ppermute | solution.py:17
  26.8 5.7 %collective-permute-start.8 = (f32[2,1,32,128]{3,2,1,0:T(8,128)S(1)}, f32[2,1,32,128]{3,2,1,0:T(8,128)S(1)}, u32[]{:S(2)}, u32[]{:S(2)}) collective-permute-start(f32[2,1,32,128]{3,2,1,0:T(8,128)S(1)} %pad_maximum_fusion.8), channel_id=1, source_target_pairs={{0,1},{1,2},{2,3},{3,4},{4,5},{5,6},{6,7},{8,9},{9,10},{10,11},{11... | collective-permute-start | bytes 98312 | tf_op jit(solution)/shard_map/ppermute | solution.py:17
  32.6 6.1 %collective-permute-start.3 = (f32[2,1,32,128]{3,2,1,0:T(8,128)S(1)}, f32[2,1,32,128]{3,2,1,0:T(8,128)S(1)}, u32[]{:S(2)}, u32[]{:S(2)}) collective-permute-start(f32[2,1,32,128]{3,2,1,0:T(8,128)S(1)} %pad_maximum_fusion.3), channel_id=1, source_target_pairs={{1,0},{2,1},{3,2},{4,3},{5,4},{6,5},{7,6},{9,8},{10,9},{11,10},{12... | collective-permute-start | bytes 98312 | tf_op jit(solution)/shard_map/ppermute | solution.py:17
  38.8 6.4 %collective-permute-start.4 = (f32[2,1,32,128]{3,2,1,0:T(8,128)S(1)}, f32[2,1,32,128]{3,2,1,0:T(8,128)S(1)}, u32[]{:S(2)}, u32[]{:S(2)}) collective-permute-start(f32[2,1,32,128]{3,2,1,0:T(8,128)S(1)} %pad_maximum_fusion.4), channel_id=1, source_target_pairs={{0,1},{1,2},{2,3},{3,4},{4,5},{5,6},{6,7},{8,9},{9,10},{10,11},{11... | collective-permute-start | bytes 98312 | tf_op jit(solution)/shard_map/ppermute | solution.py:17
  45.4 6.1 %collective-permute-start.5 = (f32[2,1,32,128]{3,2,1,0:T(8,128)S(1)}, f32[2,1,32,128]{3,2,1,0:T(8,128)S(1)}, u32[]{:S(2)}, u32[]{:S(2)}) collective-permute-start(f32[2,1,32,128]{3,2,1,0:T(8,128)S(1)} %pad_maximum_fusion.5), channel_id=1, source_target_pairs={{1,0},{2,1},{3,2},{4,3},{5,4},{6,5},{7,6},{9,8},{10,9},{11,10},{12... | collective-permute-start | bytes 98312 | tf_op jit(solution)/shard_map/ppermute | solution.py:17
  51.6 12.5 %collective-permute-start.6 = (f32[2,1,32,128]{3,2,1,0:T(8,128)S(1)}, f32[2,1,32,128]{3,2,1,0:T(8,128)S(1)}, u32[]{:S(2)}, u32[]{:S(2)}) collective-permute-start(f32[2,1,32,128]{3,2,1,0:T(8,128)S(1)} %pad_maximum_fusion.6), channel_id=1, source_target_pairs={{0,1},{1,2},{2,3},{3,4},{4,5},{5,6},{6,7},{8,9},{9,10},{10,11},{11... | collective-permute-start | bytes 98312 | tf_op jit(solution)/shard_map/ppermute | solution.py:17
  56.6 8.9 %collective-permute-start.10 = (f32[2,1,32,128]{3,2,1,0:T(8,128)S(1)}, f32[2,1,32,128]{3,2,1,0:T(8,128)S(1)}, u32[]{:S(2)}, u32[]{:S(2)}) collective-permute-start(f32[2,1,32,128]{3,2,1,0:T(8,128)S(1)} %pad_maximum_fusion.10), channel_id=1, source_target_pairs={{1,0},{2,1},{3,2},{4,3},{5,4},{6,5},{7,6},{9,8},{10,9},{11,10},{12... | collective-permute-start | bytes 98312 | tf_op jit(solution)/shard_map/ppermute | solution.py:17
  64.2 13.8 %collective-permute-start.7 = (f32[2,1,32,128]{3,2,1,0:T(8,128)S(1)}, f32[2,1,32,128]{3,2,1,0:T(8,128)S(1)}, u32[]{:S(2)}, u32[]{:S(2)}) collective-permute-start(f32[2,1,32,128]{3,2,1,0:T(8,128)S(1)} %pad_maximum_fusion.7), channel_id=1, source_target_pairs={{1,0},{2,1},{3,2},{4,3},{5,4},{6,5},{7,6},{9,8},{10,9},{11,10},{12... | collective-permute-start | bytes 98312 | tf_op jit(solution)/shard_map/ppermute | solution.py:17
  78.2 6.2 %copy-start.3 = (f32[1,4,1024]{2,1,0:T(4,128)S(1)}, f32[1,4,1024]{2,1,0:T(4,128)}, u32[]{:S(2)}) copy-start(f32[1,4,1024]{2,1,0:T(4,128)} %param.9) | copy-start | bytes 49156
  90.7 6.9 %collective-permute-start.11 = (f32[2,1,32,128]{3,2,1,0:T(8,128)S(1)}, f32[2,1,32,128]{3,2,1,0:T(8,128)S(1)}, u32[]{:S(2)}, u32[]{:S(2)}) collective-permute-start(f32[2,1,32,128]{3,2,1,0:T(8,128)S(1)} %pad_maximum_fusion.11), channel_id=1, source_target_pairs={{0,1},{1,2},{2,3},{3,4},{4,5},{5,6},{6,7},{8,9},{9,10},{10,11},{11... | collective-permute-start | bytes 98312 | tf_op jit(solution)/shard_map/ppermute | solution.py:17
  97.8 7.6 %collective-permute-start.12 = (f32[2,1,32,128]{3,2,1,0:T(8,128)S(1)}, f32[2,1,32,128]{3,2,1,0:T(8,128)S(1)}, u32[]{:S(2)}, u32[]{:S(2)}) collective-permute-start(f32[2,1,32,128]{3,2,1,0:T(8,128)S(1)} %pad_maximum_fusion.12), channel_id=1, source_target_pairs={{1,0},{2,1},{3,2},{4,3},{5,4},{6,5},{7,6},{9,8},{10,9},{11,10},{12... | collective-permute-start | bytes 98312 | tf_op jit(solution)/shard_map/ppermute | solution.py:17
  105.5 10.4 %collective-permute-start.13 = (f32[2,1,32,128]{3,2,1,0:T(8,128)S(1)}, f32[2,1,32,128]{3,2,1,0:T(8,128)S(1)}, u32[]{:S(2)}, u32[]{:S(2)}) collective-permute-start(f32[2,1,32,128]{3,2,1,0:T(8,128)S(1)} %pad_maximum_fusion.13), channel_id=1, source_target_pairs={{0,1},{1,2},{2,3},{3,4},{4,5},{5,6},{6,7},{8,9},{9,10},{10,11},{11... | collective-permute-start | bytes 98312 | tf_op jit(solution)/shard_map/ppermute | solution.py:17
  110.8 6.7 %collective-permute-start.9 = (f32[2,1,32,128]{3,2,1,0:T(8,128)S(1)}, f32[2,1,32,128]{3,2,1,0:T(8,128)S(1)}, u32[]{:S(2)}, u32[]{:S(2)}) collective-permute-start(f32[2,1,32,128]{3,2,1,0:T(8,128)S(1)} %pad_maximum_fusion.9), channel_id=1, source_target_pairs={{0,1},{1,2},{2,3},{3,4},{4,5},{5,6},{6,7},{8,9},{9,10},{10,11},{11... | collective-permute-start | bytes 98312 | tf_op jit(solution)/shard_map/ppermute | solution.py:17
  116.1 7.7 %collective-permute-start.14 = (f32[2,1,32,128]{3,2,1,0:T(8,128)S(1)}, f32[2,1,32,128]{3,2,1,0:T(8,128)S(1)}, u32[]{:S(2)}, u32[]{:S(2)}) collective-permute-start(f32[2,1,32,128]{3,2,1,0:T(8,128)S(1)} %pad_maximum_fusion.14), channel_id=1, source_target_pairs={{1,0},{2,1},{3,2},{4,3},{5,4},{6,5},{7,6},{9,8},{10,9},{11,10},{12... | collective-permute-start | bytes 98312 | tf_op jit(solution)/shard_map/ppermute | solution.py:17
  123.9 10.7 %collective-permute-start.15 = (f32[2,1,32,128]{3,2,1,0:T(8,128)S(1)}, f32[2,1,32,128]{3,2,1,0:T(8,128)S(1)}, u32[]{:S(2)}, u32[]{:S(2)}) collective-permute-start(f32[2,1,32,128]{3,2,1,0:T(8,128)S(1)} %pad_maximum_fusion.15), channel_id=1, source_target_pairs={{0,1},{1,2},{2,3},{3,4},{4,5},{5,6},{6,7},{8,9},{9,10},{10,11},{11... | collective-permute-start | bytes 98312 | tf_op jit(solution)/shard_map/ppermute | solution.py:17
  147.8 0.6 copy-start.1
where the time goes:
time: 151 us; the launch traced here: 150 us
  starting transfers between devices  56.2 us (37%)
  local copies, waits for them, and re-layouts  28.2 us (19%)
  other arithmetic  27.8 us (18%)
  waiting for transfers between devices  15.5 us (10%)
  blocking collectives  13 us (9%)
  between operations  9.11 us (6%)
    ppermute x16, starting transfers between devices, passed_along(): lax.ppermute(value, axis, [(source, source + steps) for source in range(l...  48.9 us
    gather x4, local copies, waits for them, and re-layouts, local(): traces.append(electric[0].reshape(-1)[cells])  24.6 us
    scatter-add x4, other arithmetic, local(): injected = adjoint_e[0].reshape(-1).at[cells].add(resid[STEPS - 1 - numbe...  24.4 us
    ppermute x16, waiting for transfers between devices, passed_along(): lax.ppermute(value, axis, [(source, source + steps) for source in range(l...  15.4 us
    all_to_all x1, blocking collectives, local(): lax.all_to_all(returning, ('src', 'gx'), split_axis=0, concat_axis=0, til...  13 us
    all_to_all x1, starting transfers between devices, local(): lax.all_to_all(outgoing, ('src', 'gx'), split_axis=0, concat_axis=0, tile...  7.39 us
  transfers between devices with their start and end apart: 17, of which 7 were waited for; matrix products, arithmetic and copies ran while one was open for 26% of the time, Pallas kernels for 0%

commit v1 on v0

v1 whole, which is shorter than its diff:
```python
import functools

import jax
import jax.numpy as jnp
from jax import lax
from jax.experimental import pallas as pl
from jax.experimental.pallas import tpu as pltpu
from jax.sharding import PartitionSpec as P

STEPS = 4
ROUNDS = 2 * STEPS - 1

electric_step = 0.5
magnetic_step = 0.5
loss_scale = 0.25
MESH = pl.DeviceIdType.MESH


def next_z(values):
    depth = values.shape[2]
    lane = lax.broadcasted_iota(jnp.int32, values.shape, 2)
    return jnp.where(lane == depth - 1, 0.0, pltpu.roll(values, depth - 1, 2))


def prev_z(values):
    lane = lax.broadcasted_iota(jnp.int32, values.shape, 2)
    return jnp.where(lane == 0, 0.0, pltpu.roll(values, 1, 2))


def next_y(values):
    count = values.shape[1]
    row = lax.broadcasted_iota(jnp.int32, values.shape, 1)
    return jnp.where(row == count - 1, 0.0, pltpu.roll(values, count - 1, 1))


def prev_y(values):
    row = lax.broadcasted_iota(jnp.int32, values.shape, 1)
    return jnp.where(row == 0, 0.0, pltpu.roll(values, 1, 1))


def repeat(count, body):
    if count <= 16:
        for index in range(count):
            body(index)
    else:
        pl.loop(0, count)(body)


def kernel(
    width,
    groups,
    log_ref,
    e_ref,
    offsets_ref,
    cells_ref,
    observed_ref,
    out_ref,
    model_send,
    model_recv,
    foot,
    stored,
    sources,
    to_left,
    to_right,
    from_right,
    from_left,
    padded,
    grad_send,
    grad_recv,
    model_sems,
    grad_sems,
    left_send_sems,
    left_recv_sems,
    right_send_sems,
    right_recv_sems,
):
    group = lax.axis_index("src")
    slab = lax.axis_index("gx")
    owners = groups * width
    own = group * width + slab
    planes, columns, depth = foot.shape
    model_planes, block_cols = log_ref.shape[0], log_ref.shape[1]
    blocks = columns // block_cols
    foot_x = planes * width
    room = model_planes - foot_x
    has_left = slab > 0
    has_right = slab < width - 1

    barrier = pltpu.get_barrier_semaphore()

    def greet(index):
        other = lax.rem(own + index + 1, owners)
        pl.semaphore_signal(
            barrier,
            inc=1,
            device_id={"src": other // width, "gx": lax.rem(other, width)},
            device_id_type=MESH,
        )

    repeat(owners - 1, greet)

    for source in range(groups):
        model_send[source * foot_x : (source + 1) * foot_x] = log_ref[
            pl.ds(offsets_ref[source, 0], foot_x)
        ]
    model_recv[own] = log_ref[pl.ds(offsets_ref[group, 0] + planes * slab, planes)]
    grad_recv[:, :room] = jnp.zeros((groups, room) + log_ref.shape[1:], jnp.float32)
    grad_recv[:, room + foot_x :] = jnp.zeros((groups, room) + log_ref.shape[1:], jnp.float32)
    edge = jnp.zeros((blocks, planes, block_cols, depth), jnp.float32)
    padded[:blocks] = edge
    padded[2 * blocks :] = edge

    @pl.when(jnp.logical_not(has_left))
    def _():
        from_left[...] = jnp.zeros_like(from_left)

    @pl.when(jnp.logical_not(has_right))
    def _():
        from_right[...] = jnp.zeros_like(from_right)

    def left_copy(number):
        return pltpu.make_async_remote_copy(
            src_ref=to_left.at[number],
            dst_ref=from_right.at[number],
            send_sem=left_send_sems.at[number],
            recv_sem=left_recv_sems.at[number],
            device_id={"gx": slab - 1},
            device_id_type=MESH,
        )

    def right_copy(number):
        return pltpu.make_async_remote_copy(
            src_ref=to_right.at[number],
            dst_ref=from_left.at[number],
            send_sem=right_send_sems.at[number],
            recv_sem=right_recv_sems.at[number],
            device_id={"gx": slab + 1},
            device_id_type=MESH,
        )

    def begin(number, electric, magnetic):
        ex, ey, ez = electric
        hy = magnetic[1][planes - 1 :] if magnetic is not None else 0.0
        hz = magnetic[2][planes - 1 :] if magnetic is not None else 0.0
        last_x = ex[planes - 1 :]
        part_y = hy - magnetic_step * (next_z(last_x) - last_x)
        part_z = hz + magnetic_step * (next_y(last_x) - last_x)
        if ey is not None:
            part_y = part_y - magnetic_step * ez[planes - 1 :]
            part_z = part_z + magnetic_step * ey[planes - 1 :]
            to_left[number, 0] = ey[0]
            to_left[number, 1] = ez[0]
        to_right[number, 0] = part_y[0]
        to_right[number, 1] = part_z[0]

        def send():
            if ey is not None:

                @pl.when(has_left)
                def _():
                    left_copy(number).start()

            @pl.when(has_right)
            def _():
                right_copy(number).start()

        return (part_y, part_z), send

    def finish(number, electric, magnetic, parts, coefficients):
        ex, ey, ez = electric
        part_y, part_z = parts
        damping, driving = coefficients()
        inner = magnetic is not None
        first_x = ex[: planes - 1]
        hx = magnetic[0] if inner else 0.0
        front_y = (magnetic[1][: planes - 1] if inner else 0.0) - magnetic_step * (
            next_z(first_x) - first_x
        )
        front_z = (magnetic[2][: planes - 1] if inner else 0.0) + magnetic_step * (
            next_y(first_x) - first_x
        )
        if ey is not None:
            hx = hx - magnetic_step * ((next_y(ez) - ez) - (next_z(ey) - ey))
            front_y = front_y + magnetic_step * (ez[1:] - ez[: planes - 1])
            front_z = front_z - magnetic_step * (ey[1:] - ey[: planes - 1])

            @pl.when(has_right)
            def _():
                left_copy(number).wait_recv()

            part_y = part_y + magnetic_step * from_right[number, 1][None]
            part_z = part_z - magnetic_step * from_right[number, 0][None]
        hy = jnp.concatenate([front_y, part_y], 0)
        hz = jnp.concatenate([front_z, part_z], 0)

        @pl.when(has_left)
        def _():
            right_copy(number).wait_recv()

        ghost_y = from_left[number, 0][None]
        ghost_z = from_left[number, 1][None]
        if ey is not None:
            ghost_y = ghost_y + jnp.where(has_left, magnetic_step * ez[:1], 0.0)
            ghost_z = ghost_z - jnp.where(has_left, magnetic_step * ey[:1], 0.0)
        back_y = hy - jnp.concatenate([ghost_y, hy[: planes - 1]], 0)
        back_z = hz - jnp.concatenate([ghost_z, hz[: planes - 1]], 0)
        new_x = damping * ex + driving * ((hz - prev_y(hz)) - (hy - prev_z(hy)))
        if ey is None:
            hx = jnp.zeros_like(hy)
            new_y = driving * (-back_z)
            new_z = driving * back_y
        else:
            new_y = damping * ey + driving * ((hx - prev_z(hx)) - back_z)
            new_z = damping * ez + driving * (back_y - (hx - prev_y(hx)))
        return (new_x, new_y, new_z), (hx, hy, hz)

    def model_copy(index):
        other = lax.rem(own + index + 1, owners)
        return pltpu.make_async_remote_copy(
            src_ref=model_send.at[pl.ds(planes * other, planes)],
            dst_ref=model_recv.at[own],
            send_sem=model_sems.at[0],
            recv_sem=model_sems.at[1],
            device_id={"src": other // width, "gx": lax.rem(other, width)},
            device_id_type=MESH,
        )

    def grad_copy(index):
        other = lax.rem(own + index + 1, owners)
        return pltpu.make_async_remote_copy(
            src_ref=grad_send.at[other],
            dst_ref=grad_recv.at[group, pl.ds(room + planes * slab, planes)],
            send_sem=grad_sems.at[0],
            recv_sem=grad_sems.at[1],
            device_id={"src": other // width, "gx": lax.rem(other, width)},
            device_id_type=MESH,
        )

    electric = (e_ref[0, 0], e_ref[0, 1], e_ref[0, 2])
    magnetic = None
    parts, send = begin(0, electric, magnetic)
    pl.semaphore_wait(barrier, owners - 1)
    send()
    repeat(owners - 1, lambda index: model_copy(index).start())

    cells = cells_ref[...]
    receivers = cells.shape[1]
    row_of = lax.div(cells, depth)
    lane_of = lax.rem(cells, depth)
    lane_hot = (
        lax.broadcasted_iota(jnp.int32, (depth, receivers), 0) == lane_of
    ).astype(jnp.float32).astype(jnp.bfloat16)
    values = []
    rest = observed_ref[0]
    for _ in range(3):
        piece = rest.astype(jnp.bfloat16).astype(jnp.float32)
        rest = rest - piece
        values.append(piece)
    rows = 64

    def scatter(chunk):
        hot = lax.broadcasted_iota(jnp.int32, (rows, receivers), 0) + chunk * rows == row_of
        stack = [hot.astype(jnp.float32).astype(jnp.bfloat16)]
        for number in range(STEPS):
            for piece in values:
                stack.append(
                    jnp.where(hot, piece[number : number + 1], 0.0).astype(jnp.bfloat16)
                )
        summed = lax.dot_general(
            jnp.concatenate(stack, 0),
            lane_hot,
            (((1,), (1,)), ((), ())),
            preferred_element_type=jnp.float32,
        )
        place = pl.ds(chunk * rows, rows)
        sources[0, place] = summed[:rows]
        for number in range(STEPS):
            base = rows * (1 + 3 * number)
            sources[1 + number, place] = (
                summed[base + 2 * rows : base + 3 * rows]
                + summed[base + rows : base + 2 * rows]
                + summed[base : base + rows]
            )

    repeat(planes * columns // rows, scatter)

    my_block = offsets_ref[group, 1]

    def arrived(sems, buffer, slot):
        whole = buffer.at[pl.ds(0, owners - 1)]
        pltpu.make_async_copy(whole, whole, sems.at[slot]).wait()

    held = []

    def coefficients():
        if not held:
            arrived(model_sems, model_recv, 1)
            for block in range(blocks):
                foot[:, block * block_cols : (block + 1) * block_cols] = model_recv[
                    my_block + block
                ]
            sigma = jnp.exp(foot[...])
            absorb = loss_scale * sigma
            driving = electric_step / (1.0 + absorb)
            held.append((sigma, (1.0 - absorb) / (1.0 + absorb), driving))
        return held[0][1:]

    def source_of(number, field):
        shape = (planes, columns, depth)
        return sources[0].reshape(shape) * field - sources[number].reshape(shape)

    for number in range(STEPS):
        if number:
            parts, send = begin(number, electric, magnetic)
            send()
        electric, magnetic = finish(number, electric, magnetic, parts, coefficients)
        for part in range(3):
            stored[number, part] = electric[part]

    adjoint = (source_of(STEPS, electric[0]), None, None)
    magnetic = None
    total = adjoint[0] * electric[0]
    for number in range(1, STEPS):
        turn = STEPS + number - 1
        paired = STEPS - 1 - number
        parts, send = begin(turn, adjoint, magnetic)
        send()
        adjoint, magnetic = finish(turn, adjoint, magnetic, parts, coefficients)
        adjoint = (adjoint[0] + source_of(paired + 1, stored[paired, 0]),) + adjoint[1:]
        total = total + (
            adjoint[0] * stored[paired, 0]
            + adjoint[1] * stored[paired, 1]
            + adjoint[2] * stored[paired, 2]
        )

    foot[...] = held[0][0] * total
    for block in range(blocks):
        padded[blocks + block] = foot[:, block * block_cols : (block + 1) * block_cols]
    grad_send[...] = padded[pl.ds(blocks - my_block, owners)]
    repeat(owners - 1, lambda index: grad_copy(index).start())
    grad_recv[group, pl.ds(room + planes * slab, planes)] = grad_send[own]

    arrived(model_sems, model_recv, 0)
    for number in range(ROUNDS):
        if number != STEPS:

            @pl.when(has_left)
            def _():
                left_copy(number).wait_send()

        @pl.when(has_right)
        def _():
            right_copy(number).wait_send()

    arrived(grad_sems, grad_send, 0)
    arrived(grad_sems, grad_send, 1)
    result = grad_recv[0, pl.ds(room - offsets_ref[0, 0], model_planes)]
    for source in range(1, groups):
        result = result + grad_recv[source, pl.ds(room - offsets_ref[source, 0], model_planes)]
    out_ref[...] = result


def local(log_cond, e_start, offsets, rec_cells, observed):
    groups = offsets.shape[0]
    width = lax.axis_size("gx")
    owners = groups * width
    planes, columns, depth = e_start.shape[2:]
    model_planes, block_cols = log_cond.shape[:2]
    blocks = columns // block_cols
    foot_x = planes * width
    room = model_planes - foot_x
    vmem = pl.BlockSpec(memory_space=pltpu.VMEM)
    smem = pl.BlockSpec(memory_space=pltpu.SMEM)
    piece = (planes, block_cols, depth)
    plane = (columns, depth)
    halo = pltpu.VMEM((ROUNDS, 2) + plane, jnp.float32)
    scratch = [
        pltpu.VMEM((groups * foot_x, block_cols, depth), jnp.float32),
        pltpu.VMEM((owners,) + piece, jnp.float32),
        pltpu.VMEM((planes, columns, depth), jnp.float32),
        pltpu.VMEM((STEPS, 3, planes, columns, depth), jnp.float32),
        pltpu.VMEM((STEPS + 1, planes * columns, depth), jnp.float32),
        halo,
        halo,
        halo,
        halo,
        pltpu.VMEM((3 * blocks,) + piece, jnp.float32),
        pltpu.VMEM((owners,) + piece, jnp.float32),
        pltpu.VMEM((groups, model_planes + room, block_cols, depth), jnp.float32),
        pltpu.SemaphoreType.DMA((2,)),
        pltpu.SemaphoreType.DMA((2,)),
    ] + [pltpu.SemaphoreType.DMA((ROUNDS,))] * 4
    return pl.pallas_call(
        functools.partial(kernel, width, groups),
        out_shape=jax.ShapeDtypeStruct(log_cond.shape, jnp.float32),
        in_specs=[vmem, vmem, smem, vmem, vmem],
        out_specs=vmem,
        scratch_shapes=scratch,
        compiler_params=pltpu.CompilerParams(
            collective_id=0, has_side_effects=True, vmem_limit_bytes=56 * 1024 * 1024
        ),
    )(log_cond, e_start, offsets, rec_cells, observed)


def solution(mesh):
    placed = (
        P("inv", ("src", "gx"), None),
        P("src", "inv", "gx", None, None),
        P(),
        P("src", "gx"),
        P("src", "inv", "gx"),
    )
    return jax.shard_map(
        local, mesh=mesh, in_specs=placed, out_specs=P("inv", ("src", "gx"), None), check_vma=False
    )
```

time: 151 us -> 38.9 us (0.26)
  starting transfers between devices: 56.2 us -> 0 us
  Pallas kernels: 0 us -> 37.3 us
  other arithmetic: 27.8 us -> 0 us
  local copies, waits for them, and re-layouts: 28.2 us -> 1.47 us
  waiting for transfers between devices: 15.5 us -> 0 us
  blocking collectives: 13 us -> 0 us
  between operations: 9.11 us -> 0.01 us
    ppermute x16 -> x0, starting transfers between devices: 48.9 us -> none  [passed_along(): lax.ppermute(value, axis, [(source, source + steps) for source in range(l...]
    pallas_call x0 -> x1, Pallas kernels: none -> 37.3 us  [local(): pl.pallas_call(functools.partial(kernel, width, groups), out_shape=jax.Sh...]
    gather x4 -> x0, local copies, waits for them, and re-layouts: 24.6 us -> none  [local(): traces.append(electric[0].reshape(-1)[cells])]
    scatter-add x4 -> x0, other arithmetic: 24.4 us -> none  [local(): injected = adjoint_e[0].reshape(-1).at[cells].add(resid[STEPS - 1 - numbe...]
    ppermute x16 -> x0, waiting for transfers between devices: 15.4 us -> none  [passed_along(): lax.ppermute(value, axis, [(source, source + steps) for source in range(l...]
    all_to_all x1 -> x0, blocking collectives: 13 us -> none  [local(): lax.all_to_all(returning, ('src', 'gx'), split_axis=0, concat_axis=0, til...]
    all_to_all x1 -> x0, starting transfers between devices: 7.39 us -> none  [local(): lax.all_to_all(outgoing, ('src', 'gx'), split_axis=0, concat_axis=0, tile...]
    slice x50 -> x0, local copies, waits for them, and re-layouts: 2.75 us -> none  [the longest x1 1.52 us: local(): start_block = offsets[source, 1]]
  transfers between devices with their start and end apart: 17 -> 0, of which waited for: 7 -> 0; matrix products, arithmetic and copies ran while one was open for 26% -> 0% of each run, Pallas kernels for 0% -> 0%
where the time goes in v1:
time: 38.9 us; the launch traced here: 38.8 us
  Pallas kernels  37.3 us (96%)
  local copies, waits for them, and re-layouts  1.47 us (4%)
    pallas_call x1, Pallas kernels, local(): pl.pallas_call(functools.partial(kernel, width, groups), out_shape=jax.Sh...  37.3 us
    unnamed x1, local copies, waits for them, and re-layouts  1.47 us

profile of v1, /device:TPU:0, one launch (start us, length us, event | category | flops | bytes accessed | tf_op | source)
XLA Modules:
  0.0 38.8 jit_solution(3696721447166045164)
XLA Ops:
  0.0 37.3 %shard_map.55 = f32[32,4,128]{2,1,0:T(4,128)} custom-call(f32[32,4,128]{2,1,0:T(4,128)} %log_ref.1, f32[1,3,2,32,128]{4,3,2,1,0:T(8,128)} %e_ref.1, s32[2,2]{1,0:T(2,128)} %offsets_ref.1, s32[1,1024]{1,0:T(1,128)} %cells_ref.1, f32[1,4,1024]{2,1,0:T(4,128)} %observed_ref.1), custom_call_target="tpu_custom_call" | custom-call | tf_op jit(solution)/shard_map/pallas_call | solution.py:393
  37.3 1.5 %copy.7 = f32[32,4,128]{2,1,0:T(4,128)} copy(f32[32,4,128]{2,1,0:T(4,128)} %shard_map.55) | data formatting | bytes 131072

commit v2 on v1

v2 whole, which is shorter than its diff:
```python
import functools

import jax
import jax.numpy as jnp
from jax import lax
from jax.experimental import pallas as pl
from jax.experimental.pallas import tpu as pltpu
from jax.sharding import PartitionSpec as P

STEPS = 4

electric_step = 0.5
magnetic_step = 0.5
loss_scale = 0.25
MESH = pl.DeviceIdType.MESH


def next_z(values):
    depth = values.shape[1]
    lane = lax.broadcasted_iota(jnp.int32, values.shape, 1)
    return jnp.where(lane == depth - 1, 0.0, pltpu.roll(values, depth - 1, 1))


def prev_z(values):
    lane = lax.broadcasted_iota(jnp.int32, values.shape, 1)
    return jnp.where(lane == 0, 0.0, pltpu.roll(values, 1, 1))


def next_y(values):
    count = values.shape[0]
    row = lax.broadcasted_iota(jnp.int32, values.shape, 0)
    return jnp.where(row == count - 1, 0.0, pltpu.roll(values, count - 1, 0))


def prev_y(values):
    row = lax.broadcasted_iota(jnp.int32, values.shape, 0)
    return jnp.where(row == 0, 0.0, pltpu.roll(values, 1, 0))


def repeat(count, body):
    if count <= 16:
        for index in range(count):
            body(index)
    else:
        pl.loop(0, count)(body)


def kernel(
    width,
    groups,
    log_ref,
    e_ref,
    offsets_ref,
    cells_ref,
    observed_ref,
    out_ref,
    model_send,
    model_recv,
    foot,
    stored,
    sources,
    resid,
    far_e,
    near_foot,
    far_foot,
    left_two,
    left_resid,
    right_three,
    right_four,
    far_four,
    shaped,
    padded,
    grad_send,
    grad_recv,
    model_sems,
    grad_sems,
    send_sems,
    recv_sems,
):
    group = lax.axis_index("src")
    slab = lax.axis_index("gx")
    owners = groups * width
    own = group * width + slab
    planes, columns, depth = foot.shape
    model_planes, block_cols = log_ref.shape[0], log_ref.shape[1]
    blocks = columns // block_cols
    foot_x = planes * width
    room = model_planes - foot_x

    barrier = pltpu.get_barrier_semaphore()

    def greet(index):
        other = lax.rem(own + index + 1, owners)
        pl.semaphore_signal(
            barrier,
            inc=1,
            device_id={"src": other // width, "gx": lax.rem(other, width)},
            device_id_type=MESH,
        )

    repeat(owners - 1, greet)

    for source in range(groups):
        model_send[source * foot_x : (source + 1) * foot_x] = log_ref[
            pl.ds(offsets_ref[source, 0], foot_x)
        ]
    model_recv[own] = log_ref[pl.ds(offsets_ref[group, 0] + planes * slab, planes)]
    grad_recv[:, :room] = jnp.zeros((groups, room) + log_ref.shape[1:], jnp.float32)
    grad_recv[:, room + foot_x :] = jnp.zeros((groups, room) + log_ref.shape[1:], jnp.float32)
    edge = jnp.zeros((blocks, planes, block_cols, depth), jnp.float32)
    padded[:blocks] = edge
    padded[2 * blocks :] = edge

    def apart(steps):
        return (slab + steps >= 0) & (slab + steps < width)

    def channel(number, steps, src, dst):
        copy = pltpu.make_async_remote_copy(
            src_ref=src,
            dst_ref=dst,
            send_sem=send_sems.at[number],
            recv_sem=recv_sems.at[number],
            device_id={"gx": slab + steps},
            device_id_type=MESH,
        )

        def start():
            pl.when(apart(steps))(copy.start)

        def arrive():
            pl.when(apart(-steps))(copy.wait_recv)

        def drain():
            pl.when(apart(steps))(copy.wait_send)

        return start, arrive, drain

    sides = (-1, 1, -2, 2)
    field_ways = [channel(k, sides[k], e_ref.at[0], far_e.at[k]) for k in range(4)]
    foot_ways = [
        channel(4, -1, foot, near_foot.at[0]),
        channel(5, 1, foot, near_foot.at[1]),
        channel(6, -2, foot.at[0], far_foot.at[0]),
        channel(7, 2, foot.at[1], far_foot.at[1]),
    ]
    resid_ways = {
        2: [channel(8, 1, resid.at[0, 1], left_two)],
        3: [
            channel(9, 1, resid.at[1], left_resid.at[0]),
            channel(10, -1, resid.at[1, 0], right_three),
        ],
        4: [
            channel(11, 1, resid.at[2], left_resid.at[1]),
            channel(12, -1, resid.at[2], right_four),
            channel(13, 2, resid.at[2, 1], far_four),
        ],
    }

    @pl.when(slab < 1)
    def _():
        far_e[1] = jnp.zeros_like(far_e[1])
        near_foot[1] = jnp.zeros_like(near_foot[1])
        left_two[...] = jnp.zeros_like(left_two)
        left_resid[...] = jnp.zeros_like(left_resid)

    @pl.when(slab < 2)
    def _():
        far_e[3] = jnp.zeros_like(far_e[3])
        far_foot[1] = jnp.zeros_like(far_foot[1])
        far_four[...] = jnp.zeros_like(far_four)

    @pl.when(slab >= width - 1)
    def _():
        far_e[0] = jnp.zeros_like(far_e[0])
        near_foot[0] = jnp.zeros_like(near_foot[0])
        right_three[...] = jnp.zeros_like(right_three)
        right_four[...] = jnp.zeros_like(right_four)

    @pl.when(slab >= width - 2)
    def _():
        far_e[2] = jnp.zeros_like(far_e[2])
        far_foot[0] = jnp.zeros_like(far_foot[0])

    def inside(plane):
        place = slab * planes + plane
        return (place >= 0) & (place < foot_x)

    def advance(electric, magnetic, reach, damping, driving):
        later_h = {}
        for p in range(-reach - 1, planes + reach):
            ex, ey, ez = electric[p]
            after = electric[p + 1]
            hx, hy, hz = magnetic[p] if magnetic is not None else (0.0, 0.0, 0.0)
            step = magnetic_step if p >= 0 else jnp.where(inside(p), magnetic_step, 0.0)
            curl_y = next_z(ex) - ex
            curl_z = ex - next_y(ex)
            curl_x = None
            if ey is not None:
                curl_x = (next_y(ez) - ez) - (next_z(ey) - ey)
                curl_y = curl_y + ez
                curl_z = curl_z - ey
            if after[1] is not None:
                curl_y = curl_y - after[2]
                curl_z = curl_z + after[1]
            later_h[p] = (
                jnp.zeros_like(ex) if curl_x is None else hx - step * curl_x,
                hy - step * curl_y,
                hz - step * curl_z,
            )
        later_e = {}
        for p in range(-reach, planes + reach):
            hx, hy, hz = later_h[p]
            before = later_h[p - 1]
            ex, ey, ez = electric[p]
            new_y = driving[p] * ((hx - prev_z(hx)) - (hz - before[2]))
            new_z = driving[p] * ((hy - before[1]) - (hx - prev_y(hx)))
            new_x = driving[p] * ((hz - prev_y(hz)) - (hy - prev_z(hy)))
            if ex is not None:
                new_x = damping[p] * ex + new_x
            if ey is not None:
                new_y = damping[p] * ey + new_y
                new_z = damping[p] * ez + new_z
            later_e[p] = (new_x, new_y, new_z)
        return later_e, later_h

    def model_copy(index):
        other = lax.rem(own + index + 1, owners)
        return pltpu.make_async_remote_copy(
            src_ref=model_send.at[pl.ds(planes * other, planes)],
            dst_ref=model_recv.at[own],
            send_sem=model_sems.at[0],
            recv_sem=model_sems.at[1],
            device_id={"src": other // width, "gx": lax.rem(other, width)},
            device_id_type=MESH,
        )

    def grad_copy(index):
        other = lax.rem(own + index + 1, owners)
        return pltpu.make_async_remote_copy(
            src_ref=grad_send.at[other],
            dst_ref=grad_recv.at[group, pl.ds(room + planes * slab, planes)],
            send_sem=grad_sems.at[0],
            recv_sem=grad_sems.at[1],
            device_id={"src": other // width, "gx": lax.rem(other, width)},
            device_id_type=MESH,
        )

    pl.semaphore_wait(barrier, owners - 1)
    repeat(owners - 1, lambda index: model_copy(index).start())
    for way in field_ways:
        way[0]()

    cells = cells_ref[...]
    receivers = cells.shape[1]
    row_of = lax.div(cells, depth)
    lane_of = lax.rem(cells, depth)
    lane_hot = (
        lax.broadcasted_iota(jnp.int32, (depth, receivers), 0) == lane_of
    ).astype(jnp.float32).astype(jnp.bfloat16)
    values = []
    rest = observed_ref[0]
    for _ in range(3):
        piece = rest.astype(jnp.bfloat16).astype(jnp.float32)
        rest = rest - piece
        values.append(piece)
    rows = 64

    def scatter(chunk):
        hot = lax.broadcasted_iota(jnp.int32, (rows, receivers), 0) + chunk * rows == row_of
        stack = [hot.astype(jnp.float32).astype(jnp.bfloat16)]
        for number in range(STEPS):
            for piece in values:
                stack.append(
                    jnp.where(hot, piece[number : number + 1], 0.0).astype(jnp.bfloat16)
                )
        summed = lax.dot_general(
            jnp.concatenate(stack, 0),
            lane_hot,
            (((1,), (1,)), ((), ())),
            preferred_element_type=jnp.float32,
        )
        place = pl.ds(chunk * rows, rows)
        sources[0, place] = summed[:rows]
        for number in range(STEPS):
            base = rows * (1 + 3 * number)
            sources[1 + number, place] = (
                summed[base + 2 * rows : base + 3 * rows]
                + summed[base + rows : base + 2 * rows]
                + summed[base : base + rows]
            )

    repeat(planes * columns // rows, scatter)

    my_block = offsets_ref[group, 1]

    def arrived(sems, buffer, slot):
        whole = buffer.at[pl.ds(0, owners - 1)]
        pltpu.make_async_copy(whole, whole, sems.at[slot]).wait()

    arrived(model_sems, model_recv, 1)
    for block in range(blocks):
        foot[:, block * block_cols : (block + 1) * block_cols] = model_recv[my_block + block]
    for way in foot_ways:
        way[0]()

    damping = {}
    driving = {}
    sigma = {}

    def set_coefficients(plane, value):
        level = jnp.exp(value)
        absorb = loss_scale * level
        drive = electric_step / (1.0 + absorb)
        damp = (1.0 - absorb) / (1.0 + absorb)
        if plane < 0 or plane >= planes:
            drive = jnp.where(inside(plane), drive, 0.0)
            damp = jnp.where(inside(plane), damp, 0.0)
        sigma[plane] = level
        damping[plane] = damp
        driving[plane] = drive

    for p in range(planes):
        set_coefficients(p, foot[p])
    for way in foot_ways:
        way[1]()
    for p in range(planes):
        set_coefficients(p - planes, near_foot[1, p])
        set_coefficients(p + planes, near_foot[0, p])
    set_coefficients(-planes - 1, far_foot[1])
    set_coefficients(2 * planes, far_foot[0])
    for way in field_ways:
        way[1]()
    electric = {}
    for p in range(planes):
        electric[p] = tuple(e_ref[0, part, p] for part in range(3))
        for k in range(4):
            electric[p - sides[k] * planes] = tuple(far_e[k, part, p] for part in range(3))

    def source_of(number, plane, field):
        place = slice(plane * columns, (plane + 1) * columns)
        return sources[0, place] * field - sources[number, place]

    magnetic = None
    for number in range(1, STEPS + 1):
        electric, magnetic = advance(electric, magnetic, STEPS - number, damping, driving)
        if number > 1:
            for p in range(planes):
                resid[number - 2, p] = source_of(number, p, electric[p][0])
            for way in resid_ways[number]:
                way[0]()
        if number < STEPS:
            for p in range(planes):
                for part in range(3):
                    stored[number - 1, part, p] = electric[p][part]

    total = [resid[2, p] * electric[p][0] for p in range(planes)]
    for ways in resid_ways.values():
        for way in ways:
            way[1]()
    adjoint = {
        -3: (far_four[...], None, None),
        -2: (left_resid[1, 0], None, None),
        -1: (left_resid[1, 1], None, None),
        0: (resid[2, 0], None, None),
        1: (resid[2, 1], None, None),
        2: (right_four[0], None, None),
        3: (right_four[1], None, None),
        4: (None, None, None),
    }
    injected = {
        2: {
            -2: left_resid[0, 0],
            -1: left_resid[0, 1],
            0: resid[1, 0],
            1: resid[1, 1],
            2: right_three[...],
        },
        3: {-1: left_two[...], 0: resid[0, 0], 1: resid[0, 1]},
        4: {p: source_of(1, p, stored[0, 0, p]) for p in range(planes)},
    }
    magnetic = None
    for number in range(2, STEPS + 1):
        adjoint, magnetic = advance(adjoint, magnetic, STEPS - number, damping, driving)
        for p, value in injected[number].items():
            adjoint[p] = (adjoint[p][0] + value,) + adjoint[p][1:]
        for p in range(planes):
            for part in range(3):
                total[p] = total[p] + adjoint[p][part] * stored[STEPS - number, part, p]

    for p in range(planes):
        shaped[p] = sigma[p] * total[p]
    for block in range(blocks):
        padded[blocks + block] = shaped[:, block * block_cols : (block + 1) * block_cols]
    grad_send[...] = padded[pl.ds(blocks - my_block, owners)]
    repeat(owners - 1, lambda index: grad_copy(index).start())
    grad_recv[group, pl.ds(room + planes * slab, planes)] = grad_send[own]

    arrived(model_sems, model_recv, 0)
    for way in field_ways + foot_ways + sum(resid_ways.values(), []):
        way[2]()
    arrived(grad_sems, grad_send, 0)
    arrived(grad_sems, grad_send, 1)
    result = grad_recv[0, pl.ds(room - offsets_ref[0, 0], model_planes)]
    for source in range(1, groups):
        result = result + grad_recv[source, pl.ds(room - offsets_ref[source, 0], model_planes)]
    out_ref[...] = result


def local(log_cond, e_start, offsets, rec_cells, observed):
    groups = offsets.shape[0]
    width = lax.axis_size("gx")
    owners = groups * width
    planes, columns, depth = e_start.shape[2:]
    model_planes, block_cols = log_cond.shape[:2]
    blocks = columns // block_cols
    foot_x = planes * width
    room = model_planes - foot_x
    vmem = pl.BlockSpec(memory_space=pltpu.VMEM)
    smem = pl.BlockSpec(memory_space=pltpu.SMEM)
    piece = (planes, block_cols, depth)
    plane = (columns, depth)

    def vmem_of(*shape):
        return pltpu.VMEM(shape, jnp.float32)

    scratch = [
        pltpu.VMEM((groups * foot_x, block_cols, depth), jnp.float32),
        pltpu.VMEM((owners,) + piece, jnp.float32),
        pltpu.VMEM((planes, columns, depth), jnp.float32),
        pltpu.VMEM((STEPS - 1, 3, planes, columns, depth), jnp.float32),
        pltpu.VMEM((STEPS + 1, planes * columns, depth), jnp.float32),
        vmem_of(3, planes, *plane),
        vmem_of(4, 3, planes, *plane),
        vmem_of(2, planes, *plane),
        vmem_of(2, *plane),
        vmem_of(*plane),
        vmem_of(2, planes, *plane),
        vmem_of(*plane),
        vmem_of(planes, *plane),
        vmem_of(*plane),
        vmem_of(planes, *plane),
        pltpu.VMEM((3 * blocks,) + piece, jnp.float32),
        pltpu.VMEM((owners,) + piece, jnp.float32),
        pltpu.VMEM((groups, model_planes + room, block_cols, depth), jnp.float32),
        pltpu.SemaphoreType.DMA((2,)),
        pltpu.SemaphoreType.DMA((2,)),
        pltpu.SemaphoreType.DMA((14,)),
        pltpu.SemaphoreType.DMA((14,)),
    ]
    return pl.pallas_call(
        functools.partial(kernel, width, groups),
        out_shape=jax.ShapeDtypeStruct(log_cond.shape, jnp.float32),
        in_specs=[vmem, vmem, smem, vmem, vmem],
        out_specs=vmem,
        scratch_shapes=scratch,
        compiler_params=pltpu.CompilerParams(
            collective_id=0, has_side_effects=True, vmem_limit_bytes=56 * 1024 * 1024
        ),
    )(log_cond, e_start, offsets, rec_cells, observed)


def solution(mesh):
    placed = (
        P("inv", ("src", "gx"), None),
        P("src", "inv", "gx", None, None),
        P(),
        P("src", "gx"),
        P("src", "inv", "gx"),
    )
    return jax.shard_map(
        local, mesh=mesh, in_specs=placed, out_specs=P("inv", ("src", "gx"), None), check_vma=False
    )
```

time: 38.9 us -> 26.6 us (0.68)
  Pallas kernels: 37.3 us -> 24.9 us
    pallas_call x1, Pallas kernels: 37.3 us -> 24.9 us  [local(): pl.pallas_call(functools.partial(kernel, width, groups), out_shape=jax.Sh...]
where the time goes in v2:
time: 26.6 us; the launch traced here: 26.4 us
  Pallas kernels  24.9 us (94%)
  local copies, waits for them, and re-layouts  1.47 us (6%)
    pallas_call x1, Pallas kernels, local(): pl.pallas_call(functools.partial(kernel, width, groups), out_shape=jax.Sh...  24.9 us
    unnamed x1, local copies, waits for them, and re-layouts  1.47 us

profile of v2, /device:TPU:0, one launch (start us, length us, event | category | flops | bytes accessed | tf_op | source)
XLA Modules:
  0.0 26.4 jit_solution(401057375217847747)
XLA Ops:
  0.0 24.9 %shard_map.55 = f32[32,4,128]{2,1,0:T(4,128)} custom-call(f32[32,4,128]{2,1,0:T(4,128)} %log_ref.1, f32[1,3,2,32,128]{4,3,2,1,0:T(8,128)} %e_ref.1, s32[2,2]{1,0:T(2,128)} %offsets_ref.1, s32[1,1024]{1,0:T(1,128)} %cells_ref.1, f32[1,4,1024]{2,1,0:T(4,128)} %observed_ref.1), custom_call_target="tpu_custom_call" | custom-call | tf_op jit(solution)/shard_map/pallas_call | solution.py:450
  24.9 1.5 %copy.7 = f32[32,4,128]{2,1,0:T(4,128)} copy(f32[32,4,128]{2,1,0:T(4,128)} %shard_map.55) | data formatting | bytes 131072

commit v3 on v2

--- a/solution.py
+++ b/solution.py
@@ -48,12 +48,18 @@
 def kernel(
     width,
     groups,
+    log_in,
+    e_in,
+    offsets_in,
+    cells_in,
+    observed_in,
+    out_ref,
     log_ref,
     e_ref,
     offsets_ref,
     cells_ref,
     observed_ref,
-    out_ref,
+    load_sems,
     model_send,
     model_recv,
     foot,
@@ -99,6 +105,22 @@
         )
 
     repeat(owners - 1, greet)
+    loads = [
+        pltpu.make_async_copy(src, dst, load_sems.at[k])
+        for k, (src, dst) in enumerate(
+            (
+                (offsets_in, offsets_ref),
+                (log_in, log_ref),
+                (e_in, e_ref),
+                (cells_in, cells_ref),
+                (observed_in, observed_ref),
+            )
+        )
+    ]
+    for load in loads:
+        load.start()
+    for load in loads[:3]:
+        load.wait()
 
     for source in range(groups):
         model_send[source * foot_x : (source + 1) * foot_x] = log_ref[
@@ -250,6 +272,8 @@
     for way in field_ways:
         way[0]()
 
+    for load in loads[3:]:
+        load.wait()
     cells = cells_ref[...]
     receivers = cells.shape[1]
     row_of = lax.div(cells, depth)
@@ -416,7 +440,6 @@
     foot_x = planes * width
     room = model_planes - foot_x
     vmem = pl.BlockSpec(memory_space=pltpu.VMEM)
-    smem = pl.BlockSpec(memory_space=pltpu.SMEM)
     piece = (planes, block_cols, depth)
     plane = (columns, depth)
 
@@ -424,6 +447,12 @@
         return pltpu.VMEM(shape, jnp.float32)
 
     scratch = [
+        pltpu.VMEM(log_cond.shape, jnp.float32),
+        pltpu.VMEM(e_start.shape, jnp.float32),
+        pltpu.SMEM(offsets.shape, jnp.int32),
+        pltpu.VMEM(rec_cells.shape, jnp.int32),
+        pltpu.VMEM(observed.shape, jnp.float32),
+        pltpu.SemaphoreType.DMA((5,)),
         pltpu.VMEM((groups * foot_x, block_cols, depth), jnp.float32),
         pltpu.VMEM((owners,) + piece, jnp.float32),
         pltpu.VMEM((planes, columns, depth), jnp.float32),
@@ -450,7 +479,7 @@
     return pl.pallas_call(
         functools.partial(kernel, width, groups),
         out_shape=jax.ShapeDtypeStruct(log_cond.shape, jnp.float32),
-        in_specs=[vmem, vmem, smem, vmem, vmem],
+        in_specs=[pl.BlockSpec(memory_space=pl.ANY)] * 5,
         out_specs=vmem,
         scratch_shapes=scratch,
         compiler_params=pltpu.CompilerParams(

time: 26.6 us -> 25.6 us (0.962)
  Pallas kernels: 24.9 us -> 23.9 us
    pallas_call x1, Pallas kernels: 24.9 us -> 23.9 us  [local(): pl.pallas_call(functools.partial(kernel, width, groups), out_shape=jax.Sh...]
where the time goes in v3:
time: 25.6 us; the launch traced here: 25.4 us
  Pallas kernels  23.9 us (93%)
  local copies, waits for them, and re-layouts  1.47 us (6%)
    pallas_call x1, Pallas kernels, local(): pl.pallas_call(functools.partial(kernel, width, groups), out_shape=jax.Sh...  23.9 us
    unnamed x1, local copies, waits for them, and re-layouts  1.47 us

profile of v3, /device:TPU:0, one launch (start us, length us, event | category | flops | bytes accessed | tf_op | source)
XLA Modules:
  0.0 25.4 jit_solution(4304295697441153895)
XLA Ops:
  0.0 23.9 %shard_map.55 = f32[32,4,128]{2,1,0:T(4,128)} custom-call(f32[32,4,128]{2,1,0:T(4,128)} %log_in.1, f32[1,3,2,32,128]{4,3,2,1,0:T(8,128)} %e_in.1, s32[2,2]{1,0:T(2,128)} %offsets_in.1, s32[1,1024]{1,0:T(1,128)} %cells_in.1, f32[1,4,1024]{2,1,0:T(4,128)} %observed_in.1), custom_call_target="tpu_custom_call" | custom-call | tf_op jit(solution)/shard_map/pallas_call | solution.py:479
  23.9 1.5 %copy.7 = f32[32,4,128]{2,1,0:T(4,128)} copy(f32[32,4,128]{2,1,0:T(4,128)} %shard_map.55) | data formatting | bytes 131072
